TPU v7x, 32 devices: a whole 2x2x4 slice. The times are simulated.
32 devices in a mesh: groups: 2 (over y), tp: 8 (over z, x), dp: 2 (over core).
Axes of the slice: x: 2, y: 2, z: 4, core: 2. Of those that a mesh axis runs over, the one named last changes fastest.
Arguments:
- activations: bfloat16 [2048, 8192], P(('groups', 'dp'), 'tp'), parts along dimension 0, may hold values from -6 to 6
- gate_weight: bfloat16 [8192, 28672], P('dp', 'tp'), may hold values from -0.0625 to 0.0625
- up_weight: bfloat16 [8192, 28672], P('dp', 'tp'), may hold values from -0.0625 to 0.0625
- out_grad: bfloat16 [2048, 8192], P(('groups', 'dp'), 'tp'), parts along dimension 0, may hold values from -6 to 6
- proj_in: bfloat16 [28672, 64], P('tp'), may hold values from -0.03125 to 0.03125
- proj_out: bfloat16 [8192, 64], P('tp'), may hold values from -0.0625 to 0.0625
- prompt_len: int32 [64], P(('groups', 'dp')), parts along dimension 0, may hold values from 1 to 16
- query_sketch: bfloat16 [8192, 4096], P(('groups', 'tp')), parts along dimension 0, may hold values from -6 to 6
- refusal_label: int32 [8192], P(('groups', 'tp')), parts along dimension 0, may hold values from 0 to 1
Outputs:
- scores: float32 [64, 4096], P(('groups', 'dp'), 'tp'), parts along dimension 0
- refusal_score: float32 [64], P(('groups', 'dp')), parts along dimension 0
There are 2 independent parts, one for each index of `groups`. A program takes and returns all parts, laid end to end along the dimension named above; an argument that names none is the same for every part. Nothing has to cross between parts.
All inputs are finite; a program needn't handle non-finite values.
Results may differ from a plain program's by a relative error of at most 0.0044.
Values may be sent and summed in bfloat16 or wider, within the bound.
A program may use at most 384 MiB of HBM per device.

v0:
```python
import jax
import jax.numpy as jnp
from jax import lax
from jax.sharding import PartitionSpec as P

R = 64
SEQ = 32
NQ = 4096


def shards(
    activations,
    gate_weight,
    up_weight,
    out_grad,
    proj_in,
    proj_out,
    prompt_len,
    query_sketch,
    refusal_label,
):
    tok_rows = activations.shape[0]
    count = tok_rows // SEQ
    scaling = 1.0 / (4.0 * R)
    label_sign = (2 * refusal_label - 1).astype(jnp.bfloat16)
    out_part = jnp.dot(out_grad, proj_out, preferred_element_type=jnp.float32)
    whole_gate, whole_up = (
        lax.all_gather(gate_weight, "dp", axis=0, tiled=True),
        lax.all_gather(up_weight, "dp", axis=0, tiled=True),
    )
    block_cols = lax.all_gather(activations, "tp", axis=1, tiled=True)
    gate_sum = jnp.dot(block_cols, whole_gate, preferred_element_type=jnp.float32)
    up_sum = jnp.dot(block_cols, whole_up, preferred_element_type=jnp.float32)
    hidden = (jax.nn.silu(gate_sum) * up_sum).astype(jnp.bfloat16)
    in_part = jnp.dot(hidden, proj_in, preferred_element_type=jnp.float32)
    out_side, in_side = lax.psum((out_part, in_part), "tp")
    response = (jnp.arange(SEQ, dtype=jnp.int32)[None, :] >= prompt_len[:, None]).astype(
        jnp.float32
    )
    masked = out_side.reshape(count, SEQ, R) * response[:, :, None]
    sketch = jnp.einsum(
        "eti,etj->eij", masked, in_side.reshape(count, SEQ, R), precision=lax.Precision.HIGHEST
    )
    sketch = sketch.reshape(count, R * R).astype(jnp.bfloat16)
    scores = (
        lax.dot_general(
            sketch, query_sketch, (((1,), (1,)), ((), ())), preferred_element_type=jnp.float32
        )
        * scaling
    )
    local_terms = jnp.dot(scores, label_sign.astype(jnp.float32), precision=lax.Precision.HIGHEST)
    refusal_score = lax.psum(local_terms, "tp")
    refusal_score = refusal_score / jnp.sqrt(jnp.float32(NQ))
    return (scores, refusal_score)


def solution(mesh):
    return jax.shard_map(
        shards,
        mesh=mesh,
        in_specs=(
            P(("groups", "dp"), "tp"),
            P("dp", "tp"),
            P("dp", "tp"),
            P(("groups", "dp"), "tp"),
            P("tp", None),
            P("tp", None),
            P(("groups", "dp")),
            P(("groups", "tp"), None),
            P(("groups", "tp")),
        ),
        out_specs=(P(("groups", "dp"), "tp"), P(("groups", "dp"))),
        check_vma=False,
    )
```

profile of v0, /device:TPU:0, one launch (start us, length us, event | category | flops | bytes accessed | tf_op | source)
XLA Modules:
  0.0 455.3 jit_solution(10002886258572699263)
XLA Ops:
  7.2 0.0 copy-start
  7.2 0.0 all-gather.4.cloned.1.call-start
  7.2 0.7 all-gather.4.cloned.1.call-update
  7.9 0.0 all-gather.6.cloned.1.call-start
  8.0 0.7 all-gather.6.cloned.1.call-update
  8.7 0.0 copy-start.3
  8.7 0.0 all-gather.8.cloned.1.call-start
  8.7 0.7 all-gather.8.cloned.1.call-update
  9.4 0.0 all-reduce.3.cloned.1.call-start
  9.5 0.0 copy-done
  9.5 0.1 copy-done.3
  9.6 1.1 fusion.6
  10.7 127.2 %all-gather.4.cloned.1.call-done = bf16[512,8192]{1,0:T(8,128)(2,1)} async-done(((bf16[512,1024]{1,0:T(8,128)(2,1)}), bf16[512,8192]{1,0:T(8,128)(2,1)}) %all-gather.4.cloned.1.call-update) | async-done | bytes 8388624 | tf_op jit(solution)/shard_map/all_gather | solution.py:31
  137.8 83.9 %all-gather.6.cloned.1.call-done = bf16[8192,3584]{1,0:T(8,128)(2,1)} async-done(((bf16[4096,3584]{1,0:T(8,128)(2,1)}), bf16[8192,3584]{1,0:T(8,128)(2,1)}) %all-gather.6.cloned.1.call-update) | async-done | bytes 58720272 | tf_op jit(solution)/shard_map/all_gather | solution.py:28
  221.8 46.0 %fusion.7 = f32[512,3584]{1,0:T(8,128)} fusion(bf16[512,8192]{1,0:T(8,128)(2,1)} %all-gather.4.cloned.1.call-done, bf16[8192,3584]{1,0:T(8,128)(2,1)} %all-gather.6.cloned.1.call-done), kind=kOutput, calls=%fused_computation.14 | convolution fusion | flops 30064771072 | bytes 74448896 | tf_op jit(solution)/shard_map/dot_general | solution.py:32
  267.8 40.9 %all-gather.8.cloned.1.call-done = bf16[8192,3584]{1,0:T(8,128)(2,1)} async-done(((bf16[4096,3584]{1,0:T(8,128)(2,1)}), bf16[8192,3584]{1,0:T(8,128)(2,1)}) %all-gather.8.cloned.1.call-update) | async-done | bytes 58720272 | tf_op jit(solution)/shard_map/all_gather | solution.py:29
  308.7 38.3 %multiply_convert_fusion.clone.4 = bf16[512,3584]{1,0:T(8,128)(2,1)S(1)} fusion(f32[512,3584]{1,0:T(8,128)} %fusion.7, bf16[512,8192]{1,0:T(8,128)(2,1)} %all-gather.4.cloned.1.call-done, bf16[8192,3584]{1,0:T(8,128)(2,1)} %all-gather.8.cloned.1.call-done), kind=kOutput, calls=%fused_computation.clone.clone.clone.1 | convolution fusion | flops 30075781120 | bytes 78118912 | tf_op jit(solution)/shard_map/dot_general | solution.py:33
  346.9 0.0 copy-done.6
  346.9 1.8 fusion
  348.7 0.0 all-reduce.3.cloned.1.call-update
  348.8 0.0 copy-done.4
  348.8 0.0 copy-done.5
  348.8 0.1 fusion.4
  348.9 73.8 %all-reduce.3.cloned.1.call-done = (f32[16,32,64]{2,1,0:T(8,128)}, f32[16,32,64]{2,1,0:T(8,128)}) async-done(((f32[16,32,64]{2,1,0:T(8,128)}, f32[16,32,64]{2,1,0:T(8,128)}), (f32[16,32,64]{2,1,0:T(8,128)}, f32[16,32,64]{2,1,0:T(8,128)})) %all-reduce.3.cloned.1.call-update) | async-done | bytes 262160 | tf_op jit(solution)/shard_map/psum | solution.py:36
  422.7 2.1 convolution_convert_fusion
  424.8 0.3 convert_element_type.23
  425.1 3.4 convolution_multiply_fusion
  428.5 0.1 convolution_bitcast_fusion
  428.6 19.6 %psum.23 = f32[16]{0:T(128)S(1)} all-reduce(f32[16]{0:T(128)S(1)} %convolution_bitcast_fusion), channel_id=1, replica_groups=mesh['groups'=2,'tp'=8,'dp'=2] {'tp'}, use_global_device_ids=true, to_apply=%region_2.3 | all-reduce | flops 16 | bytes 128 | tf_op jit(solution)/shard_map/psum | solution.py:52
  448.3 0.5 broadcast_multiply_fusion
  448.8 0.0 copy-done.2
  448.8 0.0 copy-done.1
  (7 shorter events, 0.0 us)
Async XLA Ops:
  7.2 2.3 copy-start
  7.2 130.7 %all-gather.4.cloned.1.call-start = ((), (), s32[]{:S(2)}) async-start(), calls=%async_computation | async-start | bytes 9437184 | tf_op jit(solution)/shard_map/all_gather | solution.py:31
  7.9 213.8 %all-gather.6.cloned.1.call-start = ((), (), s32[]{:S(2)}) async-start(), calls=%async_computation.1 | async-start | bytes 88080384 | tf_op jit(solution)/shard_map/all_gather | solution.py:28
  8.7 0.9 copy-start.3
  8.7 300.0 %all-gather.8.cloned.1.call-start = ((), (), s32[]{:S(2)}) async-start(), calls=%async_computation.2 | async-start | bytes 88080384 | tf_op jit(solution)/shard_map/all_gather | solution.py:29
  9.4 413.3 %all-reduce.3.cloned.1.call-start = ((), (), s32[]{:S(2)}) async-start(), calls=%async_computation.3 | async-start | bytes 1048576 | tf_op jit(solution)/shard_map/psum | solution.py:36
  267.8 79.2 %copy-start.6 = (bf16[3584,64]{0,1:T(8,128)(2,1)S(1)}, bf16[3584,64]{0,1:T(8,128)(2,1)}, u32[]{:S(2)}) copy-start(bf16[3584,64]{0,1:T(8,128)(2,1)} %param.13) | copy-start | bytes 1376260
  267.8 81.0 %copy-start.4 = (s32[512]{0:T(512)S(1)}, s32[512]{0:T(512)}, u32[]{:S(2)}) copy-start(s32[512]{0:T(512)} %param.17) | copy-start | bytes 6148
  267.8 81.0 %copy-start.5 = (s32[16]{0:T(128)S(1)}, s32[16]{0:T(128)}, u32[]{:S(2)}) copy-start(s32[16]{0:T(128)} %param.15) | copy-start | bytes 196
  308.6 140.1 %copy-start.1 = (bf16[512,1024]{1,0:T(8,128)(2,1)S(1)}, bf16[512,1024]{1,0:T(8,128)(2,1)}, u32[]{:S(2)}) copy-start(bf16[512,1024]{1,0:T(8,128)(2,1)} %param.12) | copy-start | bytes 3145732
  428.5 20.3 %copy-start.2 = (f32[16,512]{1,0:T(8,128)}, f32[16,512]{1,0:T(8,128)S(1)}, u32[]{:S(2)}) copy-start(f32[16,512]{1,0:T(8,128)S(1)} %convolution_multiply_fusion) | copy-start | bytes 98308
Sparse Core Ops, SparseCore 0:
  10.2 127.5 all-gather.3
  139.4 82.3 all-gather.5
  223.3 85.2 all-gather.7
  348.9 73.7 all-reduce.2
where the time goes:
time: 456 us; the launch traced here: 455 us
  waiting for transfers between devices  328 us (72%)
  matrix products  92.8 us (20%)
  blocking collectives  19.6 us (4%)
  between operations  13.9 us (3%)
    all_gather x1, waiting for transfers between devices, shards(): block_cols = lax.all_gather(activations, 'tp', axis=1, tiled=True)  127 us
    all_gather x1, waiting for transfers between devices, shards(): lax.all_gather(gate_weight, 'dp', axis=0, tiled=True)  83.9 us
    psum x1, waiting for transfers between devices, shards(): out_side, in_side = lax.psum((out_part, in_part), 'tp')  73.8 us
    dot_general x1, matrix products, shards(): jnp.dot(block_cols, whole_gate, preferred_element_type=jnp.float32)  46 us
    all_gather x1, waiting for transfers between devices, shards(): lax.all_gather(up_weight, 'dp', axis=0, tiled=True)  40.9 us
    dot_general x1, matrix products, shards(): up_sum = jnp.dot(block_cols, whole_up, preferred_element_type=jnp.float32)  38.3 us
    psum x1, blocking collectives, shards(): refusal_score = lax.psum(local_terms, 'tp')  19.6 us
  transfers between devices with their start and end apart: 4, of which 4 were waited for; matrix products, arithmetic and copies ran while one was open for 10% of the time, Pallas kernels for 0%

commit v1 on v0

--- a/solution.py
+++ b/solution.py
@@ -1,14 +1,370 @@
+import functools
+
 import jax
 import jax.numpy as jnp
 from jax import lax
+from jax.experimental import pallas as pl
+from jax.experimental.pallas import tpu as pltpu
 from jax.sharding import PartitionSpec as P
 
 R = 64
 SEQ = 32
 NQ = 4096
+MESH = pl.DeviceIdType.MESH
+NB = 3
+
+
+def layer_kernel(
+    nt, tn, act, gate, up, pin, outw, vin,
+    sk_out, v_out,
+    A, acc, wbuf, sendb, part, rpart, skg, vbuf,
+    rsem, xsem, zsem, isem, psem, wsem, dsem, esem, tsem, trsem, gsem, grsem, vsem, vrsem, free,
+):
+    rows, feat = act.shape
+    pr = rows // 2
+    g = lax.axis_index("groups")
+    t = lax.axis_index("tp")
+    h = lax.axis_index("dp")
+    z = t // 2
+    x = t % 2
+    u = z + h * (3 - 2 * z)
+    v1 = jnp.minimum(u, 1)
+    peer = (g, t, 1 - h)
+    own = pl.multiple_of(h * rows, rows)
+    oth = pl.multiple_of((1 - h) * rows, rows)
+
+    def at_u(uu, xx):
+        return (g, 2 * (uu + h * (3 - 2 * uu)) + xx, h)
+
+    def ring(d):
+        return (g, lax.rem(t + d, 8), h)
+
+    def wcopies(w):
+        s, j = w // (2 * nt), lax.rem(w, nt)
+        v = v1 + (s % 2) * (1 - 2 * v1)
+        kz = v + h * (1 - 2 * v)
+        kx = x + (s // 2) * (1 - 2 * x)
+        r0 = pl.multiple_of((kz * 2 + kx) * feat, feat)
+        c0 = pl.multiple_of(j * tn, tn)
+        b = lax.rem(w, NB)
+        return [
+            pltpu.make_async_copy(
+                m.at[pl.ds(r0, feat), pl.ds(c0, tn)],
+                wbuf.at[b, :, pl.ds(i * tn, tn)],
+                wsem.at[b, i],
+            )
+            for i, m in enumerate((gate, up))
+        ]
+
+    def wstart(w):
+        for c in wcopies(w):
+            c.start()
+
+    for w in range(NB - 1):
+        wstart(jnp.int32(w))
+
+    barrier = pltpu.get_barrier_semaphore()
+    for d in range(1, 8):
+        pl.semaphore_signal(barrier, inc=1, device_id=ring(d), device_id_type=MESH)
+    pl.semaphore_signal(barrier, inc=1, device_id=peer, device_id_type=MESH)
+    pl.semaphore_wait(barrier, 8)
+
+    def rcopy(src, dst, ss, rs, dev):
+        return pltpu.make_async_remote_copy(
+            src_ref=src, dst_ref=dst, send_sem=ss, recv_sem=rs, device_id=dev, device_id_type=MESH
+        )
+
+    def prow(p):
+        half = (1 - h) + (p // 2) * (2 * h - 1)
+        return pl.ds(pl.multiple_of(half * rows + (p % 2) * pr, pr), pr)
+
+    def piece(s, p):
+        return A.at[s, prow(p), :]
+
+    inner = u <= 1
+
+    def mine(i):
+        return pltpu.make_async_copy(act.at[pl.ds(i * pr, pr), :], piece(0, 2 + i), rsem.at[0, 2 + i])
+
+    def lend(i):
+        dst = A.at[0, pl.ds(pl.multiple_of(h * rows + i * pr, pr), pr), :]
+        return rcopy(act.at[pl.ds(i * pr, pr), :], dst, isem.at[i], rsem.at[0, i], peer)
+
+    @pl.when(inner)
+    def _():
+        for i in range(2):
+            mine(i).start()
+
+    @pl.when(jnp.logical_not(inner))
+    def _():
+        for i in range(2):
+            lend(i).start()
+
+    def xfwd(s, p):
+        return rcopy(
+            piece(s, p), piece(s + 2, p), xsem.at[s, p], rsem.at[s + 2, p], at_u(u, 1 - x)
+        )
+
+    def zout(s, p):
+        ds = jnp.where(u == 0, 1, 0) if s == 0 else 1
+        return rcopy(piece(s, p), piece(ds, p), zsem.at[s, p], rsem.at[ds, p], at_u(u + 1, x))
+
+    def zin(p):
+        return rcopy(piece(0, p), piece(1, p), psem.at[p], rsem.at[1, p], at_u(u - 1, x))
+
+    def out_ok(s):
+        return (u <= 2) if s == 0 else jnp.logical_and(u >= 1, u <= 2)
+
+    def arrived(s, p):
+        rcopy(piece(s, p), piece(s, p), xsem.at[0, 0], rsem.at[s, p], peer).wait_recv()
+
+    def forward(s, p):
+        arrived(s, p)
+
+        @pl.when(out_ok(s))
+        def _():
+            zout(s, p).start()
+
+        if s == 0:
+
+            @pl.when(u == 1)
+            def _():
+                zin(p).start()
+
+        xfwd(s, p).start()
+
+    for d in range(1, 8):
+        rcopy(vin, vbuf.at[d], vsem.at[d], vrsem.at[d], ring(d)).start()
+
+    part[...] = outw[...]
+
+    def wready(w):
+        for c in wcopies(w):
+            c.wait()
+
+        @pl.when(w + NB - 1 < 8 * nt)
+        def _():
+            wstart(w + NB - 1)
+
+        return lax.rem(w, NB)
+
+    def step(s, m):
+        rs = pl.ds(own if m else oth, rows)
+
+        def body(j, _):
+            b = wready((2 * s + m) * nt + j)
+            for i in range(2):
+                cs = pl.ds(i * tn, tn)
+                r = jnp.dot(A[s, rs, :], wbuf[b, :, cs], preferred_element_type=jnp.float32)
+                if s == 0:
+                    acc[j, rs, cs] = r
+                else:
+                    acc[j, rs, cs] += r
+            return 0
+
+        lax.fori_loop(0, nt, body, 0)
+
+    def dsend(j):
+        b = lax.rem(j, 2)
+        return rcopy(
+            sendb.at[b], acc.at[j, pl.ds(own, rows), :], dsem.at[b], esem.at[j], peer
+        )
+
+    for s in range(3):
+        for m in range(2):
+            for p in (2 * m, 2 * m + 1):
+                (forward if s < 2 else arrived)(s, p)
+            step(s, m)
+
+    for p in range(2):
+        arrived(3, p)
+
+    def give(j, _):
+        b = wready(6 * nt + j)
+        sb = lax.rem(j, 2)
+
+        @pl.when(j >= 2)
+        def _():
+            dsend(j - 2).wait_send()
+
+        for i in range(2):
+            cs = pl.ds(i * tn, tn)
+            sendb[sb, :, cs] = acc[j, pl.ds(oth, rows), cs] + jnp.dot(
+                A[3, pl.ds(oth, rows), :], wbuf[b, :, cs], preferred_element_type=jnp.float32
+            )
+        pl.semaphore_signal(free, inc=1, device_id=peer, device_id_type=MESH)
+        pl.semaphore_wait(free, 1)
+        dsend(j).start()
+        return 0
+
+    lax.fori_loop(0, nt, give, 0)
+    for p in range(2, 4):
+        arrived(3, p)
+
+    def take(j, _):
+        b = wready(7 * nt + j)
+        half = []
+        rcopy(
+            sendb.at[0], acc.at[j, pl.ds(oth, rows), :], dsem.at[0], esem.at[j], peer
+        ).wait_recv()
+        for i in range(2):
+            cs = pl.ds(i * tn, tn)
+            r = jnp.dot(
+                A[3, pl.ds(own, rows), :], wbuf[b, :, cs], preferred_element_type=jnp.float32
+            )
+            half.append(r + acc[j, pl.ds(own, rows), cs] + acc[j, pl.ds(oth, rows), cs])
+        gs, us = half
+        hid = (gs / (1.0 + jnp.exp(-gs)) * us).astype(jnp.bfloat16)
+        pj = pin[pl.ds(pl.multiple_of(j * tn, tn), tn), :]
+        part[...] += jnp.dot(hid, pj, preferred_element_type=jnp.float32)
+        return 0
+
+    lax.fori_loop(0, nt, take, 0)
+    for j in range(nt - 2, nt):
+        dsend(jnp.int32(j)).wait_send()
+
+    share = rows // 8
+    per = share // SEQ
+
+    def scatter(d):
+        dest = lax.rem(t + d, 8)
+        src = part.at[pl.ds(pl.multiple_of(dest * share, share), share), :]
+        return rcopy(src, rpart.at[d], tsem.at[d], trsem.at[d], ring(d))
+
+    for d in range(1, 8):
+        scatter(d).start()
+    side = part[pl.ds(pl.multiple_of(t * share, share), share), :]
+    for d in range(1, 8):
+        scatter(d).wait_recv()
+        side = side + rpart[d]
+    for e in range(per):
+        one = side[e * SEQ : (e + 1) * SEQ, :]
+        gram = lax.dot_general(
+            one, one, (((0,), (0,)), ((), ())),
+            precision=lax.Precision.HIGHEST, preferred_element_type=jnp.float32,
+        )
+        skg[t * per + e] = gram[R:, :].astype(jnp.bfloat16)
+
+    def spread(d):
+        ref = skg.at[pl.ds(t * per, per)]
+        return rcopy(ref, ref, gsem.at[d], grsem.at[d], ring(d))
+
+    def landed(d):
+        ref = skg.at[pl.ds(lax.rem(t + 8 - d, 8) * per, per)]
+        rcopy(ref, ref, gsem.at[d], grsem.at[d], ring(d)).wait_recv()
+
+    for d in range(1, 8):
+        spread(d).start()
+    total = vin[...]
+    for d in range(1, 8):
+        rcopy(vin, vbuf.at[d], vsem.at[d], vrsem.at[d], ring(d)).wait()
+        total = total + vbuf[d]
+    v_out[...] = total
+    for s in range(2):
+        for p in range(4):
+            xfwd(s, p).wait_send()
+
+            @pl.when(out_ok(s))
+            def _():
+                zout(s, p).wait_send()
+
+            if s == 0:
+
+                @pl.when(u == 1)
+                def _():
+                    zin(p).wait_send()
+
+    @pl.when(jnp.logical_not(inner))
+    def _():
+        for i in range(2):
+            lend(i).wait_send()
+
+    for d in range(1, 8):
+        scatter(d).wait_send()
+    for d in range(1, 8):
+        landed(d)
+        spread(d).wait_send()
+    sk_out[...] = skg[...]
+
+
+def layer(act, gate, up, pin, outw, vin):
+    rows, feat = act.shape
+    ff = gate.shape[1]
+    tn = 512
+    nt = ff // tn
+    count = rows // SEQ
+    dma = pltpu.SemaphoreType.DMA
+    vm = pl.BlockSpec(memory_space=pltpu.VMEM)
+    hbm = pl.BlockSpec(memory_space=pl.ANY)
+    return pl.pallas_call(
+        functools.partial(layer_kernel, nt, tn),
+        out_shape=(
+            jax.ShapeDtypeStruct((count, R, 2 * R), jnp.bfloat16),
+            jax.ShapeDtypeStruct(vin.shape, jnp.float32),
+        ),
+        in_specs=[hbm, hbm, hbm, vm, vm, vm],
+        out_specs=(vm, vm),
+        scratch_shapes=[
+            pltpu.VMEM((4, 2 * rows, feat), jnp.bfloat16),
+            pltpu.VMEM((nt, 2 * rows, 2 * tn), jnp.float32),
+            pltpu.VMEM((NB, feat, 2 * tn), jnp.bfloat16),
+            pltpu.VMEM((2, rows, 2 * tn), jnp.float32),
+            pltpu.VMEM((rows, 2 * R), jnp.float32),
+            pltpu.VMEM((8, rows // 8, 2 * R), jnp.float32),
+            pltpu.VMEM((count, R, 2 * R), jnp.bfloat16),
+            pltpu.VMEM((8,) + vin.shape, jnp.float32),
+            dma((4, 4)), dma((2, 4)), dma((2, 4)), dma((2,)), dma((4,)), dma((NB, 2)),
+            dma((2,)), dma((nt,)), dma((8,)), dma((8,)), dma((8,)), dma((8,)), dma((8,)), dma((8,)),
+            pltpu.SemaphoreType.REGULAR,
+        ],
+        compiler_params=pltpu.CompilerParams(
+            collective_id=0, has_side_effects=True, vmem_limit_bytes=58 * 1024 * 1024
+        ),
+        cost_estimate=pl.CostEstimate(
+            flops=8 * rows * gate.shape[0] * ff, bytes_accessed=8 * gate.shape[0] * ff,
+            transcendentals=rows * ff,
+        ),
+    )(act, gate, up, pin, outw, vin)
 
 
 def shards(
+    activations,
+    gate_weight,
+    up_weight,
+    out_grad,
+    proj_in,
+    proj_out,
+    prompt_len,
+    query_sketch,
+    refusal_label,
+):
+    count = activations.shape[0] // SEQ
+    scaling = 1.0 / (4.0 * R)
+    label_sign = (2 * refusal_label - 1).astype(jnp.bfloat16)
+    response = (jnp.arange(SEQ, dtype=jnp.int32)[None, :] >= prompt_len[:, None]).astype(
+        jnp.float32
+    )
+    wide_out = jnp.pad(proj_out, ((0, 0), (R, 0)))
+    wide_in = jnp.pad(proj_in, ((0, 0), (0, R)))
+    outw = jnp.dot(out_grad, wide_out, preferred_element_type=jnp.float32)
+    outw = outw * response.reshape(-1, 1)
+    vin = jnp.dot(label_sign[None, :], query_sketch, preferred_element_type=jnp.float32)
+    sk, vsum = layer(
+        activations, gate_weight, up_weight, wide_in, outw, vin.reshape(-1, 128)
+    )
+    sketch = sk[:, :, :R].reshape(count, R * R)
+    scores = (
+        lax.dot_general(
+            sketch, query_sketch, (((1,), (1,)), ((), ())), preferred_element_type=jnp.float32
+        )
+        * scaling
+    )
+    refusal_score = jnp.sum(sketch.astype(jnp.float32) * vsum.reshape(1, R * R), axis=1)
+    refusal_score = refusal_score * (scaling / NQ**0.5)
+    return (scores, refusal_score)
+
+
+def plain_shards(
     activations,
     gate_weight,
     up_weight,
@@ -55,8 +411,9 @@
 
 
 def solution(mesh):
+    body = shards if (mesh.shape["tp"], mesh.shape["dp"]) == (8, 2) else plain_shards
     return jax.shard_map(
-        shards,
+        body,
         mesh=mesh,
         in_specs=(
             P(("groups", "dp"), "tp"),

time: 456 us -> 168 us (0.37)
  waiting for transfers between devices: 328 us -> 0 us
  Pallas kernels: 0 us -> 150 us
  matrix products: 92.8 us -> 9.5 us
  blocking collectives: 19.6 us -> 0 us
  between operations: 13.9 us -> 0.67 us
    all_gather x3 -> x0, waiting for transfers between devices: 252 us -> none  [the longest x1 127 us: shards(): block_cols = lax.all_gather(activations, 'tp', axis=1, tiled=True)]
    pallas_call x0 -> x1, Pallas kernels: none -> 150 us  [layer(): pl.pallas_call(functools.partial(layer_kernel, nt, tn), out_shape=(jax.Sh...]
    dot_general x6 -> x2, matrix products: 89.5 us -> 5.49 us  [the longest x1 3.45 us: shards(): jnp.dot(label_sign[None, :], query_sketch, preferred_element_type=jnp.flo...]
    psum x1 -> x0, waiting for transfers between devices: 73.8 us -> none  [shards(): out_side, in_side = lax.psum((out_part, in_part), 'tp')]
    psum x1 -> x0, blocking collectives: 19.6 us -> none  [shards(): refusal_score = lax.psum(local_terms, 'tp')]
  transfers between devices with their start and end apart: 4 -> 0, of which waited for: 4 -> 0; matrix products, arithmetic and copies ran while one was open for 10% -> 0% of each run, Pallas kernels for 0% -> 0%
where the time goes in v1:
time: 168 us; the launch traced here: 167 us
  Pallas kernels  150 us (89%)
  matrix products  9.5 us (6%)
  local copies, waits for them, and re-layouts  4.75 us (3%)
  other arithmetic  2.41 us (1%)
    pallas_call x1, Pallas kernels, layer(): pl.pallas_call(functools.partial(layer_kernel, nt, tn), out_shape=(jax.Sh...  150 us
    dot_general x1, matrix products, shards(): lax.dot_general(sketch, query_sketch, (((1,), (1,)), ((), ())), preferred...  4 us
    dot_general x1, matrix products, shards(): jnp.dot(label_sign[None, :], query_sketch, preferred_element_type=jnp.flo...  3.45 us

profile of v1, /device:TPU:0, one launch (start us, length us, event | category | flops | bytes accessed | tf_op | source)
XLA Modules:
  0.0 167.2 jit_solution(313526666680052209)
XLA Ops:
  0.6 0.0 copy-start
  0.6 0.0 copy-start.2
  0.7 1.5 copy.11
  2.2 1.1 pad.8.pin
  3.3 0.7 fusion.5
  4.0 0.1 reshape.40
  4.1 0.0 copy-done
  4.1 2.0 %fusion.3.outw = f32[512,128]{1,0:T(8,128)} fusion(bf16[512,1024]{1,0:T(8,128)(2,1)S(1)} %copy-done, bf16[1024,64]{0,1:T(8,128)(2,1)} %param.14, f32[512]{0:T(512)S(1)} %reshape.40), kind=kOutput, calls=%fused_computation.4 | convolution fusion | flops 134283264 | bytes 1443840 | tf_op jit(solution)/shard_map/dot_general | solution.py:349
  6.2 0.0 copy-done.2
  6.2 3.4 %fusion = f32[1,32,128]{2,0,1:T(1,128)} fusion(bf16[512,1,1]{0,1,2:T(2,128)(2,1)S(1)} %reshape.41, bf16[512,4096]{1,0:T(8,128)(2,1)} %param.16), kind=kOutput, calls=%fused_computation | convolution fusion | flops 4194304 | bytes 4211712 | tf_op jit(solution)/shard_map/dot_general | solution.py:351
  9.6 0.0 copy-start.1
  9.6 149.9 %shard_map.104 = (bf16[16,64,128]{2,1,0:T(8,128)(2,1)}, f32[32,128]{1,0:T(8,128)}) custom-call(bf16[512,1024]{1,0:T(8,128)(2,1)} %act.1, bf16[4096,3584]{1,0:T(8,128)(2,1)} %gate.1, bf16[4096,3584]{1,0:T(8,128)(2,1)} %up.1, bf16[3584,128]{1,0:T(8,128)(2,1)} %pad.8.pin, f32[512,128]{1,0:T(8,128)} %fusion.3.outw, f32[32,128]{1,0:T(8,128)} %bitcast.18), custom_call_target="tpu_custom_call" | custom-call | flops 60129542144 | bytes 117440512 | tf_op jit(solution)/shard_map/pallas_call | solution.py:299
  159.5 0.8 mul.43
  160.3 1.2 multiply_reduce_fusion
  161.4 0.5 broadcast_multiply_fusion
  162.0 1.2 reshape.39
  163.2 4.0 %convolution_multiply_fusion.1 = f32[16,512]{1,0:T(8,128)} fusion(bf16[16,4096]{1,0:T(8,128)(2,1)S(1)} %reshape.39, bf16[512,4096]{1,0:T(8,128)(2,1)} %param.16), kind=kOutput, calls=%fused_computation.5 | convolution fusion | flops 67117056 | bytes 4358144 | tf_op jit(solution)/shard_map/dot_general | solution.py:357
  167.2 0.0 copy-done.1
  (2 shorter events, 0.0 us)
Async XLA Ops:
  0.6 3.5 %copy-start = (bf16[512,1024]{1,0:T(8,128)(2,1)S(1)}, bf16[512,1024]{1,0:T(8,128)(2,1)}, u32[]{:S(2)}) copy-start(bf16[512,1024]{1,0:T(8,128)(2,1)} %param.12) | copy-start | bytes 3145732
  0.6 5.5 %copy-start.2 = (s32[512]{0:T(512)S(1)}, s32[512]{0:T(512)}, u32[]{:S(2)}) copy-start(s32[512]{0:T(512)} %param.17) | copy-start | bytes 6148
  9.6 157.6 %copy-start.1 = (bf16[512,1024]{1,0:T(8,128)(2,1)S(1)}, bf16[512,1024]{1,0:T(8,128)(2,1)}, u32[]{:S(2)}) copy-start(bf16[512,1024]{1,0:T(8,128)(2,1)} %param.12) | copy-start | bytes 3145732

commit v2 on v1

--- a/solution.py
+++ b/solution.py
@@ -11,14 +11,28 @@
 SEQ = 32
 NQ = 4096
 MESH = pl.DeviceIdType.MESH
+SCHEDULE = (
+    ("pass", 0, 0),
+    ("step", 0, 0),
+    ("pass", 0, 1),
+    ("step", 0, 1),
+    ("wait", 2, 0),
+    ("step", 2, 0),
+    ("pass", 1, 0),
+    ("wait", 2, 1),
+    ("step", 2, 1),
+    ("pass", 1, 1),
+    ("step", 1, 0),
+    ("step", 1, 1),
+)
 NB = 3
 
 
 def layer_kernel(
-    nt, tn, act, gate, up, pin, outw, vin,
+    nt, tn, act, gate, up, pin, outw, query, lab,
     sk_out, v_out,
-    A, acc, wbuf, sendb, part, rpart, skg, vbuf,
-    rsem, xsem, zsem, isem, psem, wsem, dsem, esem, tsem, trsem, gsem, grsem, vsem, vrsem, free,
+    A, acc, wbuf, sendb, part, rpart, skg, vself, vbuf,
+    rsem, xsem, zsem, isem, psem, wsem, dsem, esem, tsem, trsem, gsem, grsem, vsem, vrsem, qsem, free,
 ):
     rows, feat = act.shape
     pr = rows // 2
@@ -41,9 +55,9 @@
 
     def wcopies(w):
         s, j = w // (2 * nt), lax.rem(w, nt)
-        v = v1 + (s % 2) * (1 - 2 * v1)
+        v = v1 + (s // 2) * (1 - 2 * v1)
         kz = v + h * (1 - 2 * v)
-        kx = x + (s // 2) * (1 - 2 * x)
+        kx = x + (s % 2) * (1 - 2 * x)
         r0 = pl.multiple_of((kz * 2 + kx) * feat, feat)
         c0 = pl.multiple_of(j * tn, tn)
         b = lax.rem(w, NB)
@@ -60,8 +74,17 @@
         for c in wcopies(w):
             c.start()
 
-    for w in range(NB - 1):
-        wstart(jnp.int32(w))
+    def qcopy(c):
+        nq = query.shape[0]
+        return pltpu.make_async_copy(
+            query.at[:, pl.ds(c * feat, feat)],
+            wbuf.at[1 + c // 2, pl.ds((c % 2) * nq, nq), :],
+            qsem.at[c],
+        )
+
+    for c in range(4):
+        qcopy(c).start()
+    wstart(jnp.int32(0))
 
     barrier = pltpu.get_barrier_semaphore()
     for d in range(1, 8):
@@ -133,8 +156,16 @@
 
         xfwd(s, p).start()
 
-    for d in range(1, 8):
-        rcopy(vin, vbuf.at[d], vsem.at[d], vrsem.at[d], ring(d)).start()
+    nq = query.shape[0]
+    sign = jnp.broadcast_to((2 * lab[...] - 1).astype(jnp.float32), (16, nq)).astype(jnp.bfloat16)
+    for c in range(4):
+        qcopy(c).wait()
+        chunk = wbuf[1 + c // 2, pl.ds((c % 2) * nq, nq), :]
+        signed = jnp.dot(sign, chunk, preferred_element_type=jnp.float32)
+        vself[:, pl.ds(c * feat, feat)] = signed[:1]
+    wstart(jnp.int32(1))
+    for d in range(1, 8):
+        rcopy(vself, vbuf.at[d], vsem.at[d], vrsem.at[d], ring(d)).start()
 
     part[...] = outw[...]
 
@@ -148,11 +179,11 @@
 
         return lax.rem(w, NB)
 
-    def step(s, m):
+    def step(q, s, m):
         rs = pl.ds(own if m else oth, rows)
 
         def body(j, _):
-            b = wready((2 * s + m) * nt + j)
+            b = wready((2 * q + m) * nt + j)
             for i in range(2):
                 cs = pl.ds(i * tn, tn)
                 r = jnp.dot(A[s, rs, :], wbuf[b, :, cs], preferred_element_type=jnp.float32)
@@ -170,11 +201,12 @@
             sendb.at[b], acc.at[j, pl.ds(own, rows), :], dsem.at[b], esem.at[j], peer
         )
 
-    for s in range(3):
-        for m in range(2):
+    for what, s, m in SCHEDULE:
+        if what == "step":
+            step((0, 2, 1)[s], s, m)
+        else:
             for p in (2 * m, 2 * m + 1):
-                (forward if s < 2 else arrived)(s, p)
-            step(s, m)
+                (forward if what == "pass" else arrived)(s, p)
 
     for p in range(2):
         arrived(3, p)
@@ -215,8 +247,10 @@
             half.append(r + acc[j, pl.ds(own, rows), cs] + acc[j, pl.ds(oth, rows), cs])
         gs, us = half
         hid = (gs / (1.0 + jnp.exp(-gs)) * us).astype(jnp.bfloat16)
-        pj = pin[pl.ds(pl.multiple_of(j * tn, tn), tn), :]
-        part[...] += jnp.dot(hid, pj, preferred_element_type=jnp.float32)
+        pj = pin[:, pl.ds(pl.multiple_of(j * tn, tn), tn)]
+        part[:, :R] += lax.dot_general(
+            hid, pj, (((1,), (1,)), ((), ())), preferred_element_type=jnp.float32
+        )
         return 0
 
     lax.fori_loop(0, nt, take, 0)
@@ -255,9 +289,9 @@
 
     for d in range(1, 8):
         spread(d).start()
-    total = vin[...]
-    for d in range(1, 8):
-        rcopy(vin, vbuf.at[d], vsem.at[d], vrsem.at[d], ring(d)).wait()
+    total = vself[...]
+    for d in range(1, 8):
+        rcopy(vself, vbuf.at[d], vsem.at[d], vrsem.at[d], ring(d)).wait()
         total = total + vbuf[d]
     v_out[...] = total
     for s in range(2):
@@ -287,7 +321,7 @@
     sk_out[...] = skg[...]
 
 
-def layer(act, gate, up, pin, outw, vin):
+def layer(act, gate, up, pin, outw, query, lab):
     rows, feat = act.shape
     ff = gate.shape[1]
     tn = 512
@@ -300,9 +334,9 @@
         functools.partial(layer_kernel, nt, tn),
         out_shape=(
             jax.ShapeDtypeStruct((count, R, 2 * R), jnp.bfloat16),
-            jax.ShapeDtypeStruct(vin.shape, jnp.float32),
+            jax.ShapeDtypeStruct((1, query.shape[1]), jnp.float32),
         ),
-        in_specs=[hbm, hbm, hbm, vm, vm, vm],
+        in_specs=[hbm, hbm, hbm, vm, vm, hbm, vm],
         out_specs=(vm, vm),
         scratch_shapes=[
             pltpu.VMEM((4, 2 * rows, feat), jnp.bfloat16),
@@ -312,10 +346,11 @@
             pltpu.VMEM((rows, 2 * R), jnp.float32),
             pltpu.VMEM((8, rows // 8, 2 * R), jnp.float32),
             pltpu.VMEM((count, R, 2 * R), jnp.bfloat16),
-            pltpu.VMEM((8,) + vin.shape, jnp.float32),
+            pltpu.VMEM((1, query.shape[1]), jnp.float32),
+            pltpu.VMEM((8, 1, query.shape[1]), jnp.float32),
             dma((4, 4)), dma((2, 4)), dma((2, 4)), dma((2,)), dma((4,)), dma((NB, 2)),
             dma((2,)), dma((nt,)), dma((8,)), dma((8,)), dma((8,)), dma((8,)), dma((8,)), dma((8,)),
-            pltpu.SemaphoreType.REGULAR,
+            dma((4,)), pltpu.SemaphoreType.REGULAR,
         ],
         compiler_params=pltpu.CompilerParams(
             collective_id=0, has_side_effects=True, vmem_limit_bytes=58 * 1024 * 1024
@@ -324,7 +359,7 @@
             flops=8 * rows * gate.shape[0] * ff, bytes_accessed=8 * gate.shape[0] * ff,
             transcendentals=rows * ff,
         ),
-    )(act, gate, up, pin, outw, vin)
+    )(act, gate, up, pin, outw, query, lab)
 
 
 def shards(
@@ -340,17 +375,14 @@
 ):
     count = activations.shape[0] // SEQ
     scaling = 1.0 / (4.0 * R)
-    label_sign = (2 * refusal_label - 1).astype(jnp.bfloat16)
     response = (jnp.arange(SEQ, dtype=jnp.int32)[None, :] >= prompt_len[:, None]).astype(
         jnp.float32
     )
     wide_out = jnp.pad(proj_out, ((0, 0), (R, 0)))
-    wide_in = jnp.pad(proj_in, ((0, 0), (0, R)))
     outw = jnp.dot(out_grad, wide_out, preferred_element_type=jnp.float32)
     outw = outw * response.reshape(-1, 1)
-    vin = jnp.dot(label_sign[None, :], query_sketch, preferred_element_type=jnp.float32)
     sk, vsum = layer(
-        activations, gate_weight, up_weight, wide_in, outw, vin.reshape(-1, 128)
+        activations, gate_weight, up_weight, proj_in.T, outw, query_sketch, refusal_label[None, :]
     )
     sketch = sk[:, :, :R].reshape(count, R * R)
     scores = (

time: 168 us -> 163 us (0.970)
  matrix products: 9.5 us -> 6.04 us
  local copies, waits for them, and re-layouts: 4.75 us -> 2.23 us
    dot_general x1 -> x0, matrix products: 3.45 us -> none  [shards(): jnp.dot(label_sign[None, :], query_sketch, preferred_element_type=jnp.flo...]
where the time goes in v2:
time: 163 us
  Pallas kernels  150 us (92%)
  matrix products  6.04 us (4%)
  other arithmetic  3.89 us (2%)
  local copies, waits for them, and re-layouts  2.23 us (1%)
    pallas_call x1, Pallas kernels, layer(): pl.pallas_call(functools.partial(layer_kernel, nt, tn), out_shape=(jax.Sh...  150 us
    dot_general x1, matrix products, shards(): lax.dot_general(sketch, query_sketch, (((1,), (1,)), ((), ())), preferred...  4 us

profile of v2, /device:TPU:0, one launch (start us, length us, event | category | flops | bytes accessed | tf_op | source)
XLA Modules:
  0.0 163.0 jit_solution(11393363938134859797)
XLA Ops:
  0.6 0.0 copy-start
  0.6 0.8 fusion.2
  1.5 0.1 reshape.32
  1.5 0.3 copy-done
  1.9 2.0 %fusion.outw = f32[512,128]{1,0:T(8,128)} fusion(bf16[512,1024]{1,0:T(8,128)(2,1)S(1)} %copy-done, bf16[1024,64]{0,1:T(8,128)(2,1)} %param.14, f32[512]{0:T(512)S(1)} %reshape.32), kind=kOutput, calls=%fused_computation.1 | convolution fusion | flops 134283264 | bytes 1443840 | tf_op jit(solution)/shard_map/dot_general | solution.py:382
  3.9 150.2 %shard_map.104 = (bf16[16,64,128]{2,1,0:T(8,128)(2,1)}, f32[1,4096]{1,0:T(1,128)}) custom-call(bf16[512,1024]{1,0:T(8,128)(2,1)} %act.1, bf16[4096,3584]{1,0:T(8,128)(2,1)} %gate.1, bf16[4096,3584]{1,0:T(8,128)(2,1)} %up.1, bf16[64,3584]{1,0:T(8,128)(2,1)} %bitcast.9, f32[512,128]{1,0:T(8,128)} %fusion.outw, bf16[512,4096]{1,0:T(8,128)(2,1)} %query.1, ...), custom_call_target="tpu_custom_call" | custom-call | flops 60129542144 | bytes 117440512 | tf_op jit(solution)/shard_map/pallas_call | solution.py:333
  154.1 0.5 broadcast.18
  154.6 1.4 reduce.4
  156.0 0.1 mul.35
  156.1 1.2 multiply_reduce_fusion
  157.3 0.5 broadcast_multiply_fusion
  157.8 1.2 reshape.31
  159.0 4.0 %convolution_multiply_fusion.1 = f32[16,512]{1,0:T(8,128)} fusion(bf16[16,4096]{1,0:T(8,128)(2,1)S(1)} %reshape.31, bf16[512,4096]{1,0:T(8,128)(2,1)} %query.1), kind=kOutput, calls=%fused_computation.2 | convolution fusion | flops 67117056 | bytes 4358144 | tf_op jit(solution)/shard_map/dot_general | solution.py:389
Async XLA Ops:
  0.6 1.2 copy-start
